TPU v7x, 512 devices: a whole 4x8x8 slice. The times are simulated.
512 devices in a mesh: space: 8 (over z), vel: 64 (over x, y, core).
Axes of the slice: x: 4, y: 8, z: 8, core: 2. Of those that a mesh axis runs over, the one named last changes fastest.
Arguments:
- distribution: float32 [32768, 2048], P('vel', 'space'), may hold values from 0.1 to 32, as said below
- normals: float32 [4, 3, 2048], P(None, None, 'space'), may hold values from -0.3 to 0.3
- adjacency: int32 [4, 2048], P(None, 'space'), may hold values from 0 to 2047, as said below
- send_list: int32 [8, 8, 256], P('space'), may hold values from 0 to 255
- block_counts: int32 [8, 8], P(None, 'space'), may hold values from 0 to 2, as said below
Outputs:
- relaxed: float32 [32768, 2048], P('vel', 'space')
- fields: float32 [13, 2048], P(None, 'space')
Inputs may be any that keep to these rules, and one draw needn't show every extreme that they name: `adjacency`: every entry of 256 or more names a position below 128 times the sum of block_counts over the senders to its group. `block_counts`: no group sends to itself; every other pair has at least one block; one receiving group gets 2 blocks from every other group. `distribution`: Positive.
All inputs are finite; a program needn't handle non-finite values.
Results may differ from a plain program's by a relative error of at most 0.00011.
Values sent between devices are 32-bit elements; how exact they have to be, the bound alone decides.
No kernel may reach another device: no remote copies, remote signals or barrier semaphores. Data moves between devices by JAX's collectives and lax.ppermute only.
A program may use at most 64 MiB of HBM per device.

v0:
```python
import jax
import jax.numpy as jnp
from jax import lax
from jax.sharding import PartitionSpec as P

VXY = 32
TILE = 128
BND = 256
ITERS = 2
spacing = 0.3
ellipsoid_mix = -0.25
prandtl = 0.8
visc_power = 0.26
time_step = 0.025


def sent_to_all(x, axis):
    copies = jnp.broadcast_to(x, (lax.axis_size(axis), *x.shape))
    return lax.all_to_all(copies, axis, split_axis=0, concat_axis=0, tiled=True)


def laid_out(pieces, dim):
    pieces = jnp.moveaxis(pieces, 0, dim)
    shape = pieces.shape
    return pieces.reshape(*shape[:dim], shape[dim] * shape[dim + 1], *shape[dim + 2 :])


def gather_directly(x, axis, dim):
    pieces = sent_to_all(x, axis)
    return laid_out(pieces, dim)


def of_everyone(x, axis):
    return sent_to_all(x, axis).sum(axis=0)


def velocity_nodes(vel_index, z_count):
    comp_x = (vel_index % VXY).astype(jnp.float32)
    comp_y = (vel_index // VXY % VXY).astype(jnp.float32)
    comp_z = (vel_index // (VXY * VXY)).astype(jnp.float32)
    centre = (VXY - 1) / 2.0
    return jnp.stack(
        [
            (comp_x - centre) * spacing,
            (comp_y - centre) * spacing,
            (comp_z - (z_count - 1) / 2.0) * spacing,
        ]
    )


def moment_rows(velocity):
    comp_x, comp_y, comp_z = (velocity[0], velocity[1], velocity[2])
    squared = comp_x * comp_x + comp_y * comp_y + comp_z * comp_z
    return jnp.stack(
        [
            jnp.ones_like(comp_x),
            comp_x,
            comp_y,
            comp_z,
            comp_x * comp_x,
            comp_y * comp_y,
            comp_z * comp_z,
            comp_x * comp_y,
            comp_x * comp_z,
            comp_y * comp_z,
            comp_x * squared,
            comp_y * squared,
            comp_z * squared,
        ]
    )


def quad_rows(velocity):
    comp_x, comp_y, comp_z = (velocity[0], velocity[1], velocity[2])
    return jnp.stack(
        [
            comp_x * comp_x,
            comp_y * comp_y,
            comp_z * comp_z,
            comp_x * comp_y,
            comp_x * comp_z,
            comp_y * comp_z,
            comp_x,
            comp_y,
            comp_z,
            jnp.ones_like(comp_x),
        ]
    )


def macroscopic(moments):
    density = moments[0]
    mean_x = moments[1] / density
    mean_y = moments[2] / density
    mean_z = moments[3] / density
    second = moments[4:10] / density[None, :]
    third = moments[10:13] / density[None, :]
    theta_xx = second[0] - mean_x * mean_x
    theta_yy = second[1] - mean_y * mean_y
    theta_zz = second[2] - mean_z * mean_z
    theta_xy = second[3] - mean_x * mean_y
    theta_xz = second[4] - mean_x * mean_z
    theta_yz = second[5] - mean_y * mean_z
    temper = (theta_xx + theta_yy + theta_zz) / 3.0
    trace_b = second[0] + second[1] + second[2]
    bu_x = second[0] * mean_x + second[3] * mean_y + second[4] * mean_z
    bu_y = second[3] * mean_x + second[1] * mean_y + second[5] * mean_z
    bu_z = second[4] * mean_x + second[5] * mean_y + second[2] * mean_z
    mean_sq = mean_x * mean_x + mean_y * mean_y + mean_z * mean_z
    flux_x = 0.5 * (third[0] - 2.0 * bu_x - mean_x * trace_b + 2.0 * mean_x * mean_sq)
    flux_y = 0.5 * (third[1] - 2.0 * bu_y - mean_y * trace_b + 2.0 * mean_y * mean_sq)
    flux_z = 0.5 * (third[2] - 2.0 * bu_z - mean_z * trace_b + 2.0 * mean_z * mean_sq)
    iso_part = (1.0 - ellipsoid_mix) * temper
    lam_xx = iso_part + ellipsoid_mix * theta_xx
    lam_yy = iso_part + ellipsoid_mix * theta_yy
    lam_zz = iso_part + ellipsoid_mix * theta_zz
    lam_xy = ellipsoid_mix * theta_xy
    lam_xz = ellipsoid_mix * theta_xz
    lam_yz = ellipsoid_mix * theta_yz
    cof_xx = lam_yy * lam_zz - lam_yz * lam_yz
    cof_xy = lam_yz * lam_xz - lam_xy * lam_zz
    cof_xz = lam_xy * lam_yz - lam_yy * lam_xz
    cof_yy = lam_xx * lam_zz - lam_xz * lam_xz
    cof_yz = lam_xy * lam_xz - lam_xx * lam_yz
    cof_zz = lam_xx * lam_yy - lam_xy * lam_xy
    determinant = lam_xx * cof_xx + lam_xy * cof_xy + lam_xz * cof_xz
    inv_xx = cof_xx / determinant
    inv_yy = cof_yy / determinant
    inv_zz = cof_zz / determinant
    inv_xy = cof_xy / determinant
    inv_xz = cof_xz / determinant
    inv_yz = cof_yz / determinant
    lin_x = inv_xx * mean_x + inv_xy * mean_y + inv_xz * mean_z
    lin_y = inv_xy * mean_x + inv_yy * mean_y + inv_yz * mean_z
    lin_z = inv_xz * mean_x + inv_yz * mean_y + inv_zz * mean_z
    offset = mean_x * lin_x + mean_y * lin_y + mean_z * lin_z
    collide = prandtl * density * jnp.exp(visc_power * jnp.log(temper))
    return jnp.stack(
        [
            density,
            mean_x,
            mean_y,
            mean_z,
            theta_xx,
            theta_yy,
            theta_zz,
            theta_xy,
            theta_xz,
            theta_yz,
            flux_x,
            flux_y,
            flux_z,
            inv_xx,
            inv_yy,
            inv_zz,
            2.0 * inv_xy,
            2.0 * inv_xz,
            2.0 * inv_yz,
            -2.0 * lin_x,
            -2.0 * lin_y,
            -2.0 * lin_z,
            offset,
            collide,
        ]
    )


def ghost_slots(adjacency, counts, cells, groups, slot_count):
    ends = jnp.cumsum(counts) * TILE
    starts = ends - counts * TILE
    is_local = adjacency < cells
    position = jnp.maximum(adjacency - cells, 0)
    source = jnp.sum((ends[:, None, None] <= position[None]).astype(jnp.int32), axis=0)
    source = jnp.minimum(source, groups - 1)
    group_ids = jnp.arange(groups, dtype=jnp.int32)[:, None, None]
    chosen = jnp.sum(jnp.where(group_ids == source[None], starts[:, None, None], 0), axis=0)
    slot_pos = jnp.clip(position - chosen, 0, slot_count - 1)
    return (is_local, source, slot_pos)


def relax(current, neighbours, velocity, normals, params, norm_z, equilibrium):
    gauss = params[0][None, :] * equilibrium / norm_z[None, :]
    outflow = jnp.zeros(current.shape, jnp.float32)
    inflow = jnp.zeros(current.shape, jnp.float32)
    for side in range(normals.shape[0]):
        normal_speed = (
            velocity[0][:, None] * normals[side, 0][None, :]
            + velocity[1][:, None] * normals[side, 1][None, :]
            + velocity[2][:, None] * normals[side, 2][None, :]
        )
        outflow = outflow + jnp.maximum(normal_speed, 0.0)
        inflow = inflow + jnp.minimum(normal_speed, 0.0) * neighbours[side]
    return current + time_step * (
        params[23][None, :] * (gauss - current) - outflow * current - inflow
    )


def per_device(distribution, normals, adjacency, send_list, block_counts):
    vel_local = distribution.shape[0]
    cells = distribution.shape[1]
    total_vel = vel_local * lax.axis_size("vel")
    z_count = total_vel // (VXY * VXY)
    groups = send_list.shape[1]
    slot_count = send_list.shape[2]
    vel_index = lax.axis_index("vel") * vel_local + jnp.arange(vel_local, dtype=jnp.int32)
    velocity = velocity_nodes(vel_index, z_count)
    moment_table = moment_rows(velocity)
    quad_table = quad_rows(velocity).T
    is_local, source, slot_pos = ghost_slots(
        adjacency, block_counts[:, 0], cells, groups, slot_count
    )
    ghost_index = source * slot_count + slot_pos
    local_index = jnp.where(is_local, adjacency, 0)
    list_all = gather_directly(send_list, "space", 0)
    column = lax.dynamic_index_in_dim(list_all, lax.axis_index("space"), 1, keepdims=False)
    pull_index = (jnp.arange(groups, dtype=jnp.int32)[:, None] * BND + column).reshape(-1)

    def reduce_moments(current):
        partial_value = (
            jnp.dot(
                moment_table,
                current,
                precision=lax.Precision.HIGHEST,
                preferred_element_type=jnp.float32,
            )
            / total_vel
        )
        return macroscopic(of_everyone(partial_value, "vel"))

    current = distribution
    for iteration in range(ITERS):
        params = reduce_moments(current)
        border = lax.all_gather(current, "space", axis=1, tiled=True)
        ghosts = jnp.take(border, pull_index, axis=1)
        exponent = jnp.dot(
            quad_table,
            params[13:23],
            precision=lax.Precision.HIGHEST,
            preferred_element_type=jnp.float32,
        )
        equilibrium = jnp.exp(-0.5 * exponent)
        norm_z = of_everyone(jnp.sum(equilibrium, axis=0) / total_vel, "vel")
        neighbours = [
            jnp.where(
                is_local[side][None, :],
                jnp.take(current, local_index[side], axis=1),
                jnp.take(ghosts, ghost_index[side], axis=1),
            )
            for side in range(normals.shape[0])
        ]
        current = relax(current, neighbours, velocity, normals, params, norm_z, equilibrium)
    final = reduce_moments(current)
    return (current, final[:13])


def solution(mesh):
    placed = (
        P("vel", "space"),
        P(None, None, "space"),
        P(None, "space"),
        P("space", None, None),
        P(None, "space"),
    )
    return jax.shard_map(
        per_device,
        mesh=mesh,
        in_specs=placed,
        out_specs=(P("vel", "space"), P(None, "space")),
        check_vma=False,
    )
```

profile of v0, /device:TPU:1, one launch (start us, length us, event | category | flops | bytes accessed | tf_op | source)
XLA Modules:
  0.0 278.8 jit_solution(2723023578636813399)
XLA Ops:
  7.2 2.0 copy.61
  10.7 10.9 %all-to-all-start.2 = ((s32[8,1,8,256]{3,2,1,0:T(8,128)}), s32[8,1,8,256]{3,2,1,0:T(8,128)S(1)}, u32[]{:S(2)}, u32[]{:S(2)}) async-start(s32[8,1,8,256]{3,2,1,0:T(8,128)} %broadcast_in_dim.117), calls=%async_computation.2 | async-start | bytes 131072 | tf_op jit(solution)/shard_map/all_to_all | solution.py:19
  33.4 11.1 %all-to-all-start = ((f32[64,13,256]{2,1,0:T(8,128)}), f32[64,13,256]{2,1,0:T(8,128)S(1)}, u32[]{:S(2)}, u32[]{:S(2)}) async-start(f32[64,13,256]{2,1,0:T(8,128)} %broadcast_in_dim.112), calls=%async_computation | async-start | bytes 2097152 | tf_op jit(solution)/shard_map/all_to_all | solution.py:19
  44.6 28.4 %all-to-all-done = f32[64,13,256]{2,1,0:T(8,128)S(1)} async-done(((f32[64,13,256]{2,1,0:T(8,128)}), f32[64,13,256]{2,1,0:T(8,128)S(1)}, u32[]{:S(2)}, u32[]{:S(2)}) %all-to-all-start) | async-done | bytes 852000 | tf_op jit(solution)/shard_map/all_to_all | solution.py:19
  74.6 6.2 %all-to-all-start.1 = ((f32[64,1,256]{2,1,0:T(1,128)}), f32[64,1,256]{2,1,0:T(1,128)S(1)}, u32[]{:S(2)}, u32[]{:S(2)}) async-start(f32[64,1,256]{2,1,0:T(1,128)} %broadcast_in_dim.113), calls=%async_computation.1 | async-start | bytes 131072 | tf_op jit(solution)/shard_map/all_to_all | solution.py:19
  81.1 9.5 %all-to-all-done.1 = f32[64,1,256]{2,1,0:T(1,128)S(1)} async-done(((f32[64,1,256]{2,1,0:T(1,128)}), f32[64,1,256]{2,1,0:T(1,128)S(1)}, u32[]{:S(2)}, u32[]{:S(2)}) %all-to-all-start.1) | async-done | bytes 65568 | tf_op jit(solution)/shard_map/all_to_all | solution.py:19
  90.8 11.7 %gather_fusion.1 = f32[2048,512]{1,0:T(8,128)} fusion(f32[512,2048]{0,1:T(8,128)} %all-gather.3.cloned.1.call-done, s32[2048]{0:T(1024)S(1)} %broadcast_clamp_fusion), kind=kCustom, calls=%fused_computation.1.clone | custom fusion | bytes 8396800 | tf_op jit(solution)/shard_map/jit(_take)/gather | solution.py:234
  102.5 3.8 %select_bitcast_fusion.1 = f32[512,2048]{0,1:T(8,128)} fusion(f32[2048,512]{1,0:T(8,128)} %gather_fusion.1, pred[2048]{0:T(1024)(128)(4,1)S(1)} %compare_and_fusion), kind=kLoop, calls=%fused_computation.19 | loop fusion | flops 1048576 | bytes 8390656 | tf_op jit(solution)/shard_map/jit(_take)/select_n | solution.py:234
  106.3 3.4 %gather_fusion.8 = f32[256,512]{1,0:T(8,128)S(1)} fusion(f32[512,2048]{0,1:T(8,128)} %select_bitcast_fusion.1, s32[1024]{0:T(1024)S(1)} %pad_clamp_fusion), kind=kCustom, calls=%fused_computation.13.clone | custom fusion | bytes 1049600 | tf_op jit(solution)/shard_map/jit(_take)/gather | solution.py:247
  110.7 3.4 %gather_fusion.6 = f32[256,512]{1,0:T(8,128)S(1)} fusion(f32[512,2048]{0,1:T(8,128)} %select_bitcast_fusion.1, s32[1024]{0:T(1024)S(1)} %pad_clamp_fusion.2), kind=kCustom, calls=%fused_computation.12.clone | custom fusion | bytes 1049600 | tf_op jit(solution)/shard_map/jit(_take)/gather | solution.py:247
  115.1 4.2 %gather_fusion.4 = f32[256,512]{1,0:T(8,128)} fusion(f32[512,2048]{0,1:T(8,128)} %select_bitcast_fusion.1, s32[1024]{0:T(1024)S(1)} %pad_clamp_fusion.4), kind=kCustom, calls=%fused_computation.11.clone | custom fusion | bytes 1049600 | tf_op jit(solution)/shard_map/jit(_take)/gather | solution.py:247
  119.3 2.1 copy.67
  121.4 4.2 %gather_fusion.2 = f32[256,512]{1,0:T(8,128)} fusion(f32[512,2048]{0,1:T(8,128)} %select_bitcast_fusion.1, s32[1024]{0:T(1024)S(1)} %pad_clamp_fusion.6), kind=kCustom, calls=%fused_computation.2.clone | custom fusion | bytes 1049600 | tf_op jit(solution)/shard_map/jit(_take)/gather | solution.py:247
  125.6 2.1 copy.64
  127.6 3.6 %fusion.16 = f32[512,256]{1,0:T(8,128)} fusion(f32[512,256]{1,0:T(8,128)S(1)} %copy-done.2, f32[256,512]{0,1:T(8,128)} %copy.73, f32[256,512]{0,1:T(8,128)S(1)} %copy.72, f32[256,512]{0,1:T(8,128)} %copy.70, f32[256,512]{0,1:T(8,128)S(1)} %copy.69, f32[256,512]{0,1:T(8,128)} %copy.67, f32[256,512]{0,1:T(8,128)S(1)} %copy.66, f32[256,512]{0,1:T(8,128)} %copy.64, ...), kind=kLoop, calls=%fused_computation.46 | loop fusion | flops 7733248 | bytes 5791744 | tf_op jit(solution)/shard_map/add | solution.py:193
  132.8 32.4 %all_to_all.32 = f32[64,13,256]{2,1,0:T(8,128)S(1)} all-to-all(f32[64,13,256]{2,1,0:T(8,128)S(1)} %broadcast_in_dim.126), channel_id=1, replica_groups=mesh['space'=8,'vel'=64] {'vel'}, dimensions={0} | all-to-all | bytes 1703936 | tf_op jit(solution)/shard_map/all_to_all | solution.py:19
  166.8 6.2 %all-to-all-start.4 = ((f32[64,1,256]{2,1,0:T(1,128)}), f32[64,1,256]{2,1,0:T(1,128)S(1)}, u32[]{:S(2)}, u32[]{:S(2)}) async-start(f32[64,1,256]{2,1,0:T(1,128)} %broadcast_in_dim.127), calls=%async_computation.4 | async-start | bytes 131072 | tf_op jit(solution)/shard_map/all_to_all | solution.py:19
  175.2 1.8 gather_fusion.12
  177.0 1.8 gather_fusion.9
  180.4 2.1 copy.77
  184.5 5.3 %copy.78 = f32[512,2048]{0,1:T(8,128)} copy(f32[512,2048]{1,0:T(8,128)} %all-gather.5.cloned.1.call-done) | data formatting | bytes 8388608 | tf_op jit(solution)/shard_map/all_gather | solution.py:233
  189.8 11.7 %gather_fusion.10 = f32[2048,512]{1,0:T(8,128)} fusion(f32[512,2048]{0,1:T(8,128)} %copy.78, s32[2048]{0:T(1024)S(1)} %broadcast_clamp_fusion), kind=kCustom, calls=%fused_computation.10.clone | custom fusion | bytes 8396800 | tf_op jit(solution)/shard_map/jit(_take)/gather | solution.py:234
  201.5 3.7 %select_bitcast_fusion = f32[512,2048]{0,1:T(8,128)} fusion(f32[2048,512]{1,0:T(8,128)} %gather_fusion.10, pred[2048]{0:T(1024)(128)(4,1)S(1)} %compare_and_fusion), kind=kLoop, calls=%fused_computation.18 | loop fusion | flops 1048576 | bytes 8390656 | tf_op jit(solution)/shard_map/jit(_take)/select_n | solution.py:234
  205.3 3.4 %gather_fusion.17 = f32[256,512]{1,0:T(8,128)S(1)} fusion(f32[512,2048]{0,1:T(8,128)} %select_bitcast_fusion, s32[1024]{0:T(1024)S(1)} %pad_clamp_fusion), kind=kCustom, calls=%fused_computation.17.clone | custom fusion | bytes 1049600 | tf_op jit(solution)/shard_map/jit(_take)/gather | solution.py:247
  208.7 4.2 %gather_fusion.15 = f32[256,512]{1,0:T(8,128)} fusion(f32[512,2048]{0,1:T(8,128)} %select_bitcast_fusion, s32[1024]{0:T(1024)S(1)} %pad_clamp_fusion.2), kind=kCustom, calls=%fused_computation.16.clone | custom fusion | bytes 1049600 | tf_op jit(solution)/shard_map/jit(_take)/gather | solution.py:247
  212.9 4.2 %gather_fusion.13 = f32[256,512]{1,0:T(8,128)} fusion(f32[512,2048]{0,1:T(8,128)} %select_bitcast_fusion, s32[1024]{0:T(1024)S(1)} %pad_clamp_fusion.4), kind=kCustom, calls=%fused_computation.15.clone | custom fusion | bytes 1049600 | tf_op jit(solution)/shard_map/jit(_take)/gather | solution.py:247
  217.1 4.2 %gather_fusion.11 = f32[256,512]{1,0:T(8,128)} fusion(f32[512,2048]{0,1:T(8,128)} %select_bitcast_fusion, s32[1024]{0:T(1024)S(1)} %pad_clamp_fusion.6), kind=kCustom, calls=%fused_computation.14.clone | custom fusion | bytes 1049600 | tf_op jit(solution)/shard_map/jit(_take)/gather | solution.py:247
  222.3 2.0 copy.85
  224.3 2.0 copy.82
  226.3 2.1 copy.79
  228.4 2.9 %fusion.6 = f32[512,256]{1,0:T(8,128)S(1)} fusion(f32[512,256]{1,0:T(8,128)S(1)} %copy-done.1, f32[256,512]{0,1:T(8,128)} %copy.88, f32[256,512]{0,1:T(8,128)S(1)} %copy.87, f32[256,512]{0,1:T(8,128)} %copy.85, f32[256,512]{0,1:T(8,128)S(1)} %copy.84, f32[256,512]{0,1:T(8,128)} %copy.82, f32[256,512]{0,1:T(8,128)S(1)} %copy.81, f32[256,512]{0,1:T(8,128)} %copy.79, ...), kind=kLoop, calls=%fused_computation.32 | loop fusion | flops 7733248 | bytes 5791744 | tf_op jit(solution)/shard_map/add | solution.py:193
  231.8 38.7 %all_to_all.33 = f32[64,13,256]{2,1,0:T(8,128)S(1)} all-to-all(f32[64,13,256]{2,1,0:T(8,128)S(1)} %broadcast_in_dim.128), channel_id=1, replica_groups=mesh['space'=8,'vel'=64] {'vel'}, dimensions={0} | all-to-all | bytes 1703936 | tf_op jit(solution)/shard_map/all_to_all | solution.py:19
  (136 shorter events, 28.6 us)
Async XLA Ops:
  7.2 83.6 %all-gather.3.cloned.1.call-start = ((), (), s32[]{:S(2)}) async-start(), calls=%async_computation.6 | async-start | bytes 4718592 | tf_op jit(solution)/shard_map/all_gather | solution.py:233
  9.2 18.2 %copy-start = (f32[512,256]{0,1:T(8,128)S(1)}, f32[512,256]{0,1:T(8,128)}, u32[]{:S(2)}) copy-start(f32[512,256]{0,1:T(8,128)} %copy.61) | copy-start | bytes 1572868
  10.7 21.6 %all-to-all-start.2 = ((s32[8,1,8,256]{3,2,1,0:T(8,128)}), s32[8,1,8,256]{3,2,1,0:T(8,128)S(1)}, u32[]{:S(2)}, u32[]{:S(2)}) async-start(s32[8,1,8,256]{3,2,1,0:T(8,128)} %broadcast_in_dim.117), calls=%async_computation.2 | async-start | bytes 131072 | tf_op jit(solution)/shard_map/all_to_all | solution.py:19
  31.0 13.5 %copy-start.4 = (f32[4,3,256]{2,0,1:T(4,128)S(1)}, f32[4,3,256]{2,0,1:T(4,128)}, u32[]{:S(2)}) copy-start(f32[4,3,256]{2,0,1:T(4,128)} %param.12) | copy-start | bytes 36868
  33.4 39.6 %all-to-all-start = ((f32[64,13,256]{2,1,0:T(8,128)}), f32[64,13,256]{2,1,0:T(8,128)S(1)}, u32[]{:S(2)}, u32[]{:S(2)}) async-start(f32[64,13,256]{2,1,0:T(8,128)} %broadcast_in_dim.112), calls=%async_computation | async-start | bytes 2097152 | tf_op jit(solution)/shard_map/all_to_all | solution.py:19
  74.6 16.0 %all-to-all-start.1 = ((f32[64,1,256]{2,1,0:T(1,128)}), f32[64,1,256]{2,1,0:T(1,128)S(1)}, u32[]{:S(2)}, u32[]{:S(2)}) async-start(f32[64,1,256]{2,1,0:T(1,128)} %broadcast_in_dim.113), calls=%async_computation.1 | async-start | bytes 131072 | tf_op jit(solution)/shard_map/all_to_all | solution.py:19
  80.8 103.6 %all-gather.5.cloned.1.call-start = ((), (), s32[]{:S(2)}) async-start(), calls=%async_computation.7 | async-start | bytes 4718592 | tf_op jit(solution)/shard_map/all_gather | solution.py:233
  119.3 8.4 %copy-start.2 = (f32[512,256]{1,0:T(8,128)S(1)}, f32[512,256]{1,0:T(8,128)}, u32[]{:S(2)}) copy-start(f32[512,256]{1,0:T(8,128)} %param.11) | copy-start | bytes 1572868
  131.2 41.8 %copy-start.1 = (f32[512,256]{1,0:T(8,128)S(1)}, f32[512,256]{1,0:T(8,128)}, u32[]{:S(2)}) copy-start(f32[512,256]{1,0:T(8,128)} %fusion.16) | copy-start | bytes 1572868
  166.8 16.0 %all-to-all-start.4 = ((f32[64,1,256]{2,1,0:T(1,128)}), f32[64,1,256]{2,1,0:T(1,128)S(1)}, u32[]{:S(2)}, u32[]{:S(2)}) async-start(f32[64,1,256]{2,1,0:T(1,128)} %broadcast_in_dim.127), calls=%async_computation.4 | async-start | bytes 131072 | tf_op jit(solution)/shard_map/all_to_all | solution.py:19
  231.3 40.6 %copy-start.3 = (f32[512,256]{1,0:T(8,128)}, f32[512,256]{1,0:T(8,128)S(1)}, u32[]{:S(2)}) copy-start(f32[512,256]{1,0:T(8,128)S(1)} %fusion.6) | copy-start | bytes 1572868
Sparse Core Ops, SparseCore 0:
  10.7 63.7 all-gather.2
  131.4 53.0 all-gather.4
where the time goes:
time: 280 us; the launch traced here: 279 us
  local copies, waits for them, and re-layouts  95.1 us (34%)
  blocking collectives  71.1 us (25%)
  waiting for transfers between devices  39.9 us (14%)
  starting transfers between devices  34.6 us (12%)
  other arithmetic  19 us (7%)
  between operations  14.8 us (5%)
  matrix products  4.28 us (2%)
    all_to_all x2, blocking collectives, sent_to_all(): return lax.all_to_all(copies, axis, split_axis=0, concat_axis=0, tiled=True)  71.1 us
    gather x16, local copies, waits for them, and re-layouts, per_device(): jnp.take(ghosts, ghost_index[side], axis=1)  44.5 us
    all_to_all x4, waiting for transfers between devices, sent_to_all(): return lax.all_to_all(copies, axis, split_axis=0, concat_axis=0, tiled=True)  38.3 us
    all_to_all x4, starting transfers between devices, sent_to_all(): return lax.all_to_all(copies, axis, split_axis=0, concat_axis=0, tiled=True)  34.3 us
    gather x2, local copies, waits for them, and re-layouts, per_device(): ghosts = jnp.take(border, pull_index, axis=1)  23.5 us
    gather x16, local copies, waits for them, and re-layouts, per_device(): jnp.take(current, local_index[side], axis=1)  13.9 us
    select_n x2, other arithmetic, per_device(): ghosts = jnp.take(border, pull_index, axis=1)  7.53 us
    add x2, other arithmetic, relax(): current + time_step * (params[23][None, :] * (gauss - current) - outflow...  6.51 us
  transfers between devices with their start and end apart: 6, of which 4 were waited for; matrix products, arithmetic and copies ran while one was open for 10% of the time, Pallas kernels for 0%

commit v1 on v0

--- a/solution.py
+++ b/solution.py
@@ -230,7 +230,13 @@
     current = distribution
     for iteration in range(ITERS):
         params = reduce_moments(current)
-        border = lax.all_gather(current, "space", axis=1, tiled=True)
+
+        def write_seats_all(mesh_ax, arr):
+            value_now = lax.axis_size(mesh_ax)
+            e_now = jnp.concatenate([arr] * value_now, axis=1)
+            return lax.all_to_all(e_now, mesh_ax, 1, 1, tiled=True)
+
+        border = write_seats_all("space", arr=current)
         ghosts = jnp.take(border, pull_index, axis=1)
         exponent = jnp.dot(
             quad_table,

time: 280 us -> 458 us (1.64)
  waiting for transfers between devices: 39.9 us -> 229 us
  blocking collectives: 71.1 us -> 35.4 us
  local copies, waits for them, and re-layouts: 95.1 us -> 118 us
  starting transfers between devices: 34.6 us -> 54.3 us
  between operations: 14.8 us -> 1.31 us
    all_to_all x0 -> x2, waiting for transfers between devices: none -> 169 us  [write_seats_all(): return lax.all_to_all(e_now, mesh_ax, 1, 1, tiled=True)]
    all_to_all x2 -> x1, blocking collectives: 71.1 us -> 35.4 us  [sent_to_all(): return lax.all_to_all(copies, axis, split_axis=0, concat_axis=0, tiled=True)]
    all_to_all x4 -> x5, waiting for transfers between devices: 38.3 us -> 59.4 us  [sent_to_all(): return lax.all_to_all(copies, axis, split_axis=0, concat_axis=0, tiled=True)]
    all_to_all x0 -> x3, local copies, waits for them, and re-layouts: none -> 15.3 us  [write_seats_all(): return lax.all_to_all(e_now, mesh_ax, 1, 1, tiled=True)]
    all_to_all x0 -> x2, starting transfers between devices: none -> 11.1 us  [write_seats_all(): return lax.all_to_all(e_now, mesh_ax, 1, 1, tiled=True)]
    unnamed x13 -> x28, local copies, waits for them, and re-layouts: 2.14 us -> 11.8 us
    all_to_all x4 -> x5, starting transfers between devices: 34.3 us -> 43.1 us  [sent_to_all(): return lax.all_to_all(copies, axis, split_axis=0, concat_axis=0, tiled=True)]
    all_gather x1 -> x0, local copies, waits for them, and re-layouts: 5.34 us -> none  [per_device(): border = lax.all_gather(current, 'space', axis=1, tiled=True)]
  transfers between devices with their start and end apart: 6 -> 7, of which waited for: 4 -> 7; matrix products, arithmetic and copies ran while one was open for 10% -> 10% of each run, Pallas kernels for 0% -> 0%
where the time goes in v1:
time: 458 us; the launch traced here: 456 us
  waiting for transfers between devices  229 us (50%)
  local copies, waits for them, and re-layouts  118 us (26%)
  starting transfers between devices  54.3 us (12%)
  blocking collectives  35.4 us (8%)
  other arithmetic  15.9 us (3%)
    all_to_all x2, waiting for transfers between devices, write_seats_all(): return lax.all_to_all(e_now, mesh_ax, 1, 1, tiled=True)  169 us
    all_to_all x5, waiting for transfers between devices, sent_to_all(): return lax.all_to_all(copies, axis, split_axis=0, concat_axis=0, tiled=True)  59.4 us
    all_to_all x5, starting transfers between devices, sent_to_all(): return lax.all_to_all(copies, axis, split_axis=0, concat_axis=0, tiled=True)  43.1 us
    gather x16, local copies, waits for them, and re-layouts, per_device(): jnp.take(ghosts, ghost_index[side], axis=1)  40.8 us
    all_to_all x1, blocking collectives, sent_to_all(): return lax.all_to_all(copies, axis, split_axis=0, concat_axis=0, tiled=True)  35.4 us
    gather x2, local copies, waits for them, and re-layouts, per_device(): ghosts = jnp.take(border, pull_index, axis=1)  23.4 us
    gather x16, local copies, waits for them, and re-layouts, per_device(): jnp.take(current, local_index[side], axis=1)  18.4 us
    all_to_all x3, local copies, waits for them, and re-layouts, write_seats_all(): return lax.all_to_all(e_now, mesh_ax, 1, 1, tiled=True)  15.3 us
  transfers between devices with their start and end apart: 7, of which 7 were waited for; matrix products, arithmetic and copies ran while one was open for 10% of the time, Pallas kernels for 0%

profile of v1, /device:TPU:1, one launch (start us, length us, event | category | flops | bytes accessed | tf_op | source)
XLA Modules:
  0.0 456.5 jit_solution(4173499744871663356)
XLA Ops:
  3.5 11.8 %all-to-all-start = ((f32[64,13,256]{2,1,0:T(8,128)}), f32[64,13,256]{2,1,0:T(8,128)S(1)}, u32[]{:S(2)}, u32[]{:S(2)}) async-start(f32[64,13,256]{2,1,0:T(8,128)} %broadcast_in_dim.112), calls=%async_computation | async-start | bytes 2097152 | tf_op jit(solution)/shard_map/all_to_all | solution.py:19
  20.6 23.2 %all-to-all-done = f32[64,13,256]{2,1,0:T(8,128)S(1)} async-done(((f32[64,13,256]{2,1,0:T(8,128)}), f32[64,13,256]{2,1,0:T(8,128)S(1)}, u32[]{:S(2)}, u32[]{:S(2)}) %all-to-all-start) | async-done | bytes 852000 | tf_op jit(solution)/shard_map/all_to_all | solution.py:19
  44.4 10.1 %all-to-all-start.3 = ((s32[8,1,8,256]{3,2,1,0:T(8,128)}), s32[8,1,8,256]{3,2,1,0:T(8,128)S(1)}, u32[]{:S(2)}, u32[]{:S(2)}) async-start(s32[8,1,8,256]{3,2,1,0:T(8,128)} %broadcast_in_dim.117), calls=%async_computation.3 | async-start | bytes 131072 | tf_op jit(solution)/shard_map/all_to_all | solution.py:19
  55.5 6.2 %all-to-all-done.3 = s32[8,1,8,256]{3,2,1,0:T(8,128)S(1)} async-done(((s32[8,1,8,256]{3,2,1,0:T(8,128)}), s32[8,1,8,256]{3,2,1,0:T(8,128)S(1)}, u32[]{:S(2)}, u32[]{:S(2)}) %all-to-all-start.3) | async-done | bytes 65568 | tf_op jit(solution)/shard_map/all_to_all | solution.py:19
  62.3 7.7 %all-to-all-start.1 = ((f32[64,1,256]{2,1,0:T(1,128)}), f32[64,1,256]{2,1,0:T(1,128)S(1)}, u32[]{:S(2)}, u32[]{:S(2)}) async-start(f32[64,1,256]{2,1,0:T(1,128)} %broadcast_in_dim.113), calls=%async_computation.1 | async-start | bytes 131072 | tf_op jit(solution)/shard_map/all_to_all | solution.py:19
  71.8 5.4 %copy.119 = f32[512,2048]{0,1:T(8,128)} copy(f32[512,2048]{1,0:T(8,128)} %constant_dynamic-update-slice_fusion) | data formatting | bytes 8388608 | tf_op jit(solution)/shard_map/all_to_all | solution.py:237
  77.2 2.6 all-to-all-done.1
  79.8 4.9 %all-to-all-start.2 = ((f32[512,8,256]{0,2,1:T(8,128)}), f32[512,8,256]{0,2,1:T(8,128)}, u32[]{:S(2)}, u32[]{:S(2)}) async-start(f32[512,8,256]{0,2,1:T(8,128)} %bitcast.150), calls=%async_computation.2 | async-start | bytes 8388608 | tf_op jit(solution)/shard_map/all_to_all | solution.py:237
  95.1 81.9 %all-to-all-done.2 = f32[512,8,256]{0,2,1:T(8,128)} async-done(((f32[512,8,256]{0,2,1:T(8,128)}), f32[512,8,256]{0,2,1:T(8,128)}, u32[]{:S(2)}, u32[]{:S(2)}) %all-to-all-start.2) | async-done | bytes 4194336 | tf_op jit(solution)/shard_map/all_to_all | solution.py:237
  177.0 11.7 %gather_fusion.1 = f32[2048,512]{1,0:T(8,128)} fusion(f32[512,2048]{0,1:T(8,128)} %bitcast.22, s32[2048]{0:T(1024)S(1)} %broadcast_clamp_fusion), kind=kCustom, calls=%fused_computation.1.clone | custom fusion | bytes 8396800 | tf_op jit(solution)/shard_map/jit(_take)/gather | solution.py:240
  188.8 3.8 select_bitcast_fusion.1
  192.6 3.4 gather_fusion.8
  197.0 3.4 gather_fusion.6
  201.4 3.4 gather_fusion.4
  205.8 3.4 gather_fusion.2
  210.2 3.8 constant_dynamic-update-slice_fusion.15
  215.4 7.5 %all-to-all-start.4 = ((f32[64,13,256]{2,1,0:T(8,128)}), f32[64,13,256]{2,1,0:T(8,128)S(1)}, u32[]{:S(2)}, u32[]{:S(2)}) async-start(f32[64,13,256]{2,1,0:T(8,128)} %broadcast_in_dim.126), calls=%async_computation.4 | async-start | bytes 2097152 | tf_op jit(solution)/shard_map/all_to_all | solution.py:19
  227.3 24.2 %all-to-all-done.4 = f32[64,13,256]{2,1,0:T(8,128)S(1)} async-done(((f32[64,13,256]{2,1,0:T(8,128)}), f32[64,13,256]{2,1,0:T(8,128)S(1)}, u32[]{:S(2)}, u32[]{:S(2)}) %all-to-all-start.4) | async-done | bytes 852000 | tf_op jit(solution)/shard_map/all_to_all | solution.py:19
  253.1 6.2 %all-to-all-start.5 = ((f32[64,1,256]{2,1,0:T(1,128)}), f32[64,1,256]{2,1,0:T(1,128)S(1)}, u32[]{:S(2)}, u32[]{:S(2)}) async-start(f32[64,1,256]{2,1,0:T(1,128)} %broadcast_in_dim.127), calls=%async_computation.5 | async-start | bytes 131072 | tf_op jit(solution)/shard_map/all_to_all | solution.py:19
  261.1 4.6 %copy.144 = f32[64,8,8,256]{3,2,0,1:T(8,128)} copy(f32[64,8,8,256]{3,2,1,0:T(8,128)} %bitcast.152) | data formatting | bytes 8388608 | tf_op jit(solution)/shard_map/all_to_all | solution.py:237
  265.7 3.4 all-to-all-done.5
  269.1 6.2 %all-to-all-start.6 = ((f32[512,8,256]{2,0,1:T(8,128)}), f32[512,8,256]{2,0,1:T(8,128)}, u32[]{:S(2)}, u32[]{:S(2)}) async-start(f32[512,8,256]{2,0,1:T(8,128)} %bitcast.151), calls=%async_computation.6 | async-start | bytes 8388608 | tf_op jit(solution)/shard_map/all_to_all | solution.py:237
  284.9 87.4 %all-to-all-done.6 = f32[512,8,256]{2,0,1:T(8,128)} async-done(((f32[512,8,256]{2,0,1:T(8,128)}), f32[512,8,256]{2,0,1:T(8,128)}, u32[]{:S(2)}, u32[]{:S(2)}) %all-to-all-start.6) | async-done | bytes 4194336 | tf_op jit(solution)/shard_map/all_to_all | solution.py:237
  372.3 5.4 %copy.107 = f32[512,8,256]{0,2,1:T(8,128)} copy(f32[512,8,256]{2,0,1:T(8,128)} %all-to-all-done.6) | data formatting | bytes 8388608 | tf_op jit(solution)/shard_map/all_to_all | solution.py:237
  377.6 11.7 %gather_fusion.10 = f32[2048,512]{1,0:T(8,128)} fusion(f32[512,2048]{0,1:T(8,128)} %bitcast.149, s32[2048]{0:T(1024)S(1)} %broadcast_clamp_fusion), kind=kCustom, calls=%fused_computation.10.clone | custom fusion | bytes 8396800 | tf_op jit(solution)/shard_map/jit(_take)/gather | solution.py:240
  389.3 3.8 select_bitcast_fusion
  393.1 3.4 gather_fusion.17
  396.5 4.2 gather_fusion.15
  400.7 4.2 gather_fusion.13
  404.9 4.2 gather_fusion.11
  416.2 2.9 fusion.6
  419.6 35.4 %all_to_all.56 = f32[64,13,256]{2,1,0:T(8,128)S(1)} all-to-all(f32[64,13,256]{2,1,0:T(8,128)S(1)} %broadcast_in_dim.128), channel_id=1, replica_groups=mesh['space'=8,'vel'=64] {'vel'}, dimensions={0} | all-to-all | bytes 1703936 | tf_op jit(solution)/shard_map/all_to_all | solution.py:19
  (147 shorter events, 54.1 us)
Async XLA Ops:
  0.6 14.7 %copy-start = (f32[512,256]{1,0:T(8,128)S(1)}, f32[512,256]{1,0:T(8,128)}, u32[]{:S(2)}) copy-start(f32[512,256]{1,0:T(8,128)} %param.11) | copy-start | bytes 1572868
  3.5 40.3 %copy-start.4 = (s32[1,8,256]{2,1,0:T(8,128)S(1)}, s32[1,8,256]{2,1,0:T(8,128)}, u32[]{:S(2)}) copy-start(s32[1,8,256]{2,1,0:T(8,128)} %param.14) | copy-start | bytes 24580
  3.5 40.3 %all-to-all-start = ((f32[64,13,256]{2,1,0:T(8,128)}), f32[64,13,256]{2,1,0:T(8,128)S(1)}, u32[]{:S(2)}, u32[]{:S(2)}) async-start(f32[64,13,256]{2,1,0:T(8,128)} %broadcast_in_dim.112), calls=%async_computation | async-start | bytes 2097152 | tf_op jit(solution)/shard_map/all_to_all | solution.py:19
  44.4 17.2 %all-to-all-start.3 = ((s32[8,1,8,256]{3,2,1,0:T(8,128)}), s32[8,1,8,256]{3,2,1,0:T(8,128)S(1)}, u32[]{:S(2)}, u32[]{:S(2)}) async-start(s32[8,1,8,256]{3,2,1,0:T(8,128)} %broadcast_in_dim.117), calls=%async_computation.3 | async-start | bytes 131072 | tf_op jit(solution)/shard_map/all_to_all | solution.py:19
  62.3 17.5 %all-to-all-start.1 = ((f32[64,1,256]{2,1,0:T(1,128)}), f32[64,1,256]{2,1,0:T(1,128)S(1)}, u32[]{:S(2)}, u32[]{:S(2)}) async-start(f32[64,1,256]{2,1,0:T(1,128)} %broadcast_in_dim.113), calls=%async_computation.1 | async-start | bytes 131072 | tf_op jit(solution)/shard_map/all_to_all | solution.py:19
  79.8 5.2 %copy-start.5 = (s32[8,1]{0,1:T(1,128)S(1)}, s32[8,1]{0,1:T(1,128)}, u32[]{:S(2)}) copy-start(s32[8,1]{0,1:T(1,128)} %param.15) | copy-start | bytes 100
  79.8 5.4 %copy-start.2 = (s32[4,256]{1,0:T(4,128)S(1)}, s32[4,256]{1,0:T(4,128)}, u32[]{:S(2)}) copy-start(s32[4,256]{1,0:T(4,128)} %param.13) | copy-start | bytes 12292
  79.8 97.2 %all-to-all-start.2 = ((f32[512,8,256]{0,2,1:T(8,128)}), f32[512,8,256]{0,2,1:T(8,128)}, u32[]{:S(2)}, u32[]{:S(2)}) async-start(f32[512,8,256]{0,2,1:T(8,128)} %bitcast.150), calls=%async_computation.2 | async-start | bytes 8388608 | tf_op jit(solution)/shard_map/all_to_all | solution.py:237
  89.6 5.3 %copy-start.3 = (f32[4,3,256]{2,0,1:T(4,128)S(1)}, f32[4,3,256]{2,0,1:T(4,128)}, u32[]{:S(2)}) copy-start(f32[4,3,256]{2,0,1:T(4,128)} %param.12) | copy-start | bytes 36868
  215.4 36.0 %all-to-all-start.4 = ((f32[64,13,256]{2,1,0:T(8,128)}), f32[64,13,256]{2,1,0:T(8,128)S(1)}, u32[]{:S(2)}, u32[]{:S(2)}) async-start(f32[64,13,256]{2,1,0:T(8,128)} %broadcast_in_dim.126), calls=%async_computation.4 | async-start | bytes 2097152 | tf_op jit(solution)/shard_map/all_to_all | solution.py:19
  253.1 16.0 %all-to-all-start.5 = ((f32[64,1,256]{2,1,0:T(1,128)}), f32[64,1,256]{2,1,0:T(1,128)S(1)}, u32[]{:S(2)}, u32[]{:S(2)}) async-start(f32[64,1,256]{2,1,0:T(1,128)} %broadcast_in_dim.127), calls=%async_computation.5 | async-start | bytes 131072 | tf_op jit(solution)/shard_map/all_to_all | solution.py:19
  269.1 103.2 %all-to-all-start.6 = ((f32[512,8,256]{2,0,1:T(8,128)}), f32[512,8,256]{2,0,1:T(8,128)}, u32[]{:S(2)}, u32[]{:S(2)}) async-start(f32[512,8,256]{2,0,1:T(8,128)} %bitcast.151), calls=%async_computation.6 | async-start | bytes 8388608 | tf_op jit(solution)/shard_map/all_to_all | solution.py:237
  419.1 37.3 %copy-start.1 = (f32[512,256]{1,0:T(8,128)}, f32[512,256]{1,0:T(8,128)S(1)}, u32[]{:S(2)}) copy-start(f32[512,256]{1,0:T(8,128)S(1)} %fusion.6) | copy-start | bytes 1572868
